TPU v7x, 1024 devices: a whole 4x4x32 slice. The times are simulated.
1024 devices in a mesh: row: 64 (over y_hi, z), col: 16 (over x, y_lo, core).
Axes of the slice: x: 4, y: 4 (y_hi: 2, y_lo: 2; y = y_hi * 2 + y_lo), z: 32, core: 2. Of those that a mesh axis runs over, the one named last changes fastest.
Arguments:
- trailing_inverse: bfloat16 [16384, 16384], P('row', 'col'), may hold values from -0.046875 to 0.046875
- l_panel: bfloat16 [16384, 512], P('row', 'col'), may hold values from -6 to 6
- pattern: int32 [64, 2], replicated, may hold values 0 or 1
Outputs:
- inverse_panel: float32 [16384, 512], P('row', 'col')
Inputs may be any that keep to these rules, and one draw needn't show every extreme that they name: pattern holds only 0 and 1.
All inputs are finite; a program needn't handle non-finite values.
Results may differ from a plain program's by a relative error of at most 0.0003.
Values may be sent and summed in bfloat16 or wider, within the bound.
No kernel may reach another device: no remote copies, remote signals or barrier semaphores. Data moves between devices by JAX's collectives and lax.ppermute only.
A program may use at most 32 MiB of HBM per device.

v0:
```python
import jax
import jax.numpy as jnp
from jax import lax
from jax.sharding import PartitionSpec as P

B = 256
RB = 1


def broadcast(value, axis, source):
    kept = jnp.where(lax.axis_index(axis) == source, value, 0).astype(value.dtype)
    return lax.psum(kept, axis)


def per_device(trailing_inverse, l_panel, pattern):
    grid_row = lax.axis_index("row")
    grid_col = lax.axis_index("col")
    ratio = lax.axis_size("row") // lax.axis_size("col")
    local_rows = l_panel.shape[0]
    supernodes = pattern.shape[1]
    my_pattern = lax.dynamic_slice_in_dim(pattern, grid_row * RB, RB, 0)
    full_row = lax.all_gather(l_panel, "col", axis=1, tiled=True)
    keep = my_pattern.astype(jnp.bfloat16)
    masked_row = (full_row.reshape(RB, B, supernodes, B) * keep[:, None, :, None]).reshape(
        local_rows, supernodes * B
    )
    arrived = []
    columns = []
    for turn in range(ratio):
        root = grid_col * ratio + turn
        piece = broadcast(masked_row, "row", root)
        inverse_cols = lax.dynamic_slice_in_dim(trailing_inverse, turn * local_rows, local_rows, 1)
        arrived.append(piece)
        columns.append(inverse_cols)
    stacked_panel = jnp.concatenate(arrived, 0)
    stacked_inverse = jnp.concatenate(columns, 1)
    partial_value = jnp.dot(stacked_inverse, stacked_panel, preferred_element_type=jnp.float32)
    negated = -my_pattern.astype(jnp.float32)
    signed = (partial_value.reshape(RB, B, supernodes, B) * negated[:, None, :, None]).reshape(
        local_rows, supernodes * B
    )
    return lax.psum_scatter(signed, "col", scatter_dimension=1, tiled=True)


def solution(mesh):
    return jax.shard_map(
        per_device,
        mesh=mesh,
        in_specs=(P("row", "col"), P("row", "col"), P()),
        out_specs=P("row", "col"),
        check_vma=False,
    )
```

profile of v0, /device:TPU:1, one launch (start us, length us, event | category | flops | bytes accessed | tf_op | source)
XLA Modules:
  0.0 695.9 jit_solution(16763637709172668048)
XLA Ops:
  6.5 0.0 copy-start
  6.5 0.0 all-reduce.3.cloned.1.call-start
  6.5 0.9 fusion.8
  7.5 0.1 broadcast_bitcast_fusion.1
  7.5 30.9 %all_gather.3 = bf16[256,512]{0,1:T(8,128)(2,1)S(1)} all-gather(bf16[256,32]{0,1:T(8,128)(2,1)} %param.4), channel_id=1, replica_groups=mesh['row'=64,'col'=16] {'col'}, dimensions={1}, use_global_device_ids=true | all-gather | bytes 278528 | tf_op jit(solution)/shard_map/all_gather | solution.py:22
  38.5 1.1 broadcast_select_fusion.3
  39.6 0.0 copy-start.1
  39.6 0.0 all-reduce.3.cloned.1.call-update
  39.6 0.0 reduce-scatter.2.cloned.1.call-start
  39.7 0.6 copy-done.1
  40.3 0.2 negate_reduce_fusion
  40.5 0.1 broadcast_bitcast_fusion
  40.6 541.0 %all-reduce.3.cloned.1.call-done = (bf16[256,512]{0,1:T(8,128)(2,1)}, bf16[256,512]{0,1:T(8,128)(2,1)}, bf16[256,512]{0,1:T(8,128)(2,1)}, bf16[256,512]{0,1:T(8,128)(2,1)}) async-done(((bf16[256,512]{0,1:T(8,128)(2,1)}, bf16[256,512]{0,1:T(8,128)(2,1)}, bf16[256,512]{0,1:T(8,128)(2,1)}, bf16[256,512]{0,1:T(8,128)(2,1)}), (bf16[256,512]{0,1:T(8,128)(2,1)}, bf16[256,512]{0,1:T(8,128)(2,1)}, ...) | async-done | bytes 1048592 | tf_op jit(solution)/shard_map/psum | solution.py:12
  581.6 0.0 copy-done
  581.6 2.5 fusion
  584.1 0.0 reduce-scatter.2.cloned.1.call-update
  584.1 105.0 %reduce-scatter.2.cloned.1.call-done = f32[256,32]{0,1:T(8,128)} async-done(((f32[256,512]{0,1:T(8,128)}), f32[256,32]{0,1:T(8,128)}) %reduce-scatter.2.cloned.1.call-update) | async-done | bytes 32784 | tf_op jit(solution)/shard_map/reduce_scatter | solution.py:42
  (2 shorter events, 0.0 us)
Async XLA Ops:
  6.5 575.1 %copy-start = (bf16[256,1024]{1,0:T(8,128)(2,1)S(1)}, bf16[256,1024]{1,0:T(8,128)(2,1)}, u32[]{:S(2)}) copy-start(bf16[256,1024]{1,0:T(8,128)(2,1)} %param.3) | copy-start | bytes 1572868
  6.5 575.1 %all-reduce.3.cloned.1.call-start = ((), (), s32[]{:S(2)}) async-start(), calls=%async_computation.2 | async-start | bytes 2097152 | tf_op jit(solution)/shard_map/psum | solution.py:12
  39.6 0.7 copy-start.1
  39.6 649.4 %reduce-scatter.2.cloned.1.call-start = ((), (), s32[]{:S(2)}) async-start(), calls=%async_computation.1 | async-start | bytes 557056 | tf_op jit(solution)/shard_map/reduce_scatter | solution.py:42
Sparse Core Ops, SparseCore 0:
  39.8 541.7 all-reduce.2
  585.3 103.7 reduce-scatter.1
where the time goes:
time: 696 us
  waiting for transfers between devices  646 us (93%)
  blocking collectives  30.9 us (4%)
  between operations  13.4 us (2%)
    psum x1, waiting for transfers between devices, broadcast(): return lax.psum(kept, axis)  541 us
    reduce_scatter x1, waiting for transfers between devices, per_device(): return lax.psum_scatter(signed, 'col', scatter_dimension=1, tiled=True)  105 us
    all_gather x1, blocking collectives, per_device(): full_row = lax.all_gather(l_panel, 'col', axis=1, tiled=True)  30.9 us
  transfers between devices with their start and end apart: 2, of which 2 were waited for; matrix products, arithmetic and copies ran while one was open for 0% of the time, Pallas kernels for 0%

commit v1 on v0

v1 whole, which is shorter than its diff:
```python
import jax
import jax.numpy as jnp
from jax import lax
from jax.experimental import pallas as pl
from jax.experimental.pallas import tpu as pltpu
from jax.sharding import Mesh, PartitionSpec as P

ROWS = ("half", "slab", "plane", "twin")
COLS = ("x", "y", "core")
QUAD = ("y", "core")


def product(panel_ref, inverse_ref, out_ref):
    halves, twins, quads, planes, pairs, width, order = panel_ref.shape
    total = jnp.zeros(out_ref.shape, jnp.float32)
    for half in range(halves):
        for pair in range(pairs):
            for plane in range(planes * twins):
                left = panel_ref[half, plane % twins, :, plane // twins, pair].reshape(quads * width, order)
                right = inverse_ref[half * pairs + pair, :, plane * order:(plane + 1) * order]
                total += lax.dot_general(left, right, (((1,), (1,)), ((), ())), preferred_element_type=jnp.float32)
    out_ref[...] = total


def multiply(panel, inverse):
    halves, twins, quads, planes, pairs, width, order = panel.shape
    vmem = pl.BlockSpec(memory_space=pltpu.VMEM)
    return pl.pallas_call(
        product,
        in_specs=[vmem, vmem],
        out_specs=vmem,
        out_shape=jax.ShapeDtypeStruct((quads * width, order), jnp.float32),
        cost_estimate=pl.CostEstimate(
            flops=2 * panel.size * order, bytes_accessed=2 * (panel.size + inverse.size), transcendentals=0
        ),
        compiler_params=pltpu.CompilerParams(vmem_limit_bytes=16 * 1024 * 1024),
    )(panel, inverse)


def per_device(trailing_inverse, l_panel, pattern):
    half, twin = lax.axis_index("half"), lax.axis_index("twin")
    row, col = lax.axis_index(ROWS), lax.axis_index(COLS)
    halves, slabs, planes, twins = (lax.axis_size(a) for a in ROWS)
    cols, quads = lax.axis_size(COLS), lax.axis_size(QUAD)
    pairs = slabs // quads
    order, width = l_panel.shape
    supernode = col * pattern.shape[1] // cols
    copies = jnp.broadcast_to(trailing_inverse[None], (lax.axis_size("x"),) + trailing_inverse.shape)
    inverse = lax.all_to_all(copies, "x", 0, 0)
    gathered = lax.all_gather(l_panel.T, ("slab", "plane"), axis=0)
    gathered = gathered.reshape(pairs, quads, planes, width, order)
    flags = lax.dynamic_index_in_dim(pattern, supernode, 1, keepdims=False)
    flags = flags.reshape(halves, pairs, quads, planes, twins)[half, ..., twin]
    masked = gathered * flags[..., None, None].astype(gathered.dtype)
    masked = masked.transpose(1, 2, 0, 3, 4)
    chunks = jnp.broadcast_to(masked[None], (halves * twins,) + masked.shape)
    panel = lax.all_to_all(chunks.reshape((-1,) + masked.shape[1:]), ("half", "twin") + QUAD, 0, 0)
    panel = panel.reshape((halves, twins) + masked.shape)
    partial = multiply(panel, inverse)
    shares = lax.all_to_all(partial.reshape(quads, width, order), QUAD, 0, 0)
    mine = pattern[row, supernode]
    return (jnp.sum(shares, 0) * -mine.astype(jnp.float32)).T


def solution(mesh):
    devices = mesh.devices.reshape(2, 8, 2, 2, 4, 2, 2)
    fine = Mesh(devices, ROWS + COLS)
    return jax.shard_map(
        per_device,
        mesh=fine,
        in_specs=(P(ROWS, COLS), P(ROWS, COLS), P()),
        out_specs=P(ROWS, COLS),
        check_vma=False,
    )
```

time: 696 us -> 88.6 us (0.13)
  waiting for transfers between devices: 646 us -> 2.36 us
  blocking collectives: 30.9 us -> 69.4 us
  between operations: 13.4 us -> 0.7 us
  starting transfers between devices: 0.04 us -> 9.43 us
    psum x1 -> x0, waiting for transfers between devices: 541 us -> none  [broadcast(): return lax.psum(kept, axis)]
    reduce_scatter x1 -> x0, waiting for transfers between devices: 105 us -> none  [per_device(): return lax.psum_scatter(signed, 'col', scatter_dimension=1, tiled=True)]
    all_to_all x0 -> x1, blocking collectives: none -> 26.9 us  [per_device(): lax.all_to_all(chunks.reshape((-1,) + masked.shape[1:]), ('half', 'twin')...]
    all_gather x1, blocking collectives: 30.9 us -> 42.4 us  [per_device(): gathered = lax.all_gather(l_panel.T, ('slab', 'plane'), axis=0)]
    all_to_all x0 -> x2, starting transfers between devices: none -> 9.43 us  [the longest x1 4.97 us: per_device(): inverse = lax.all_to_all(copies, 'x', 0, 0)]
  transfers between devices with their start and end apart: 2 -> 2, of which waited for: 2 -> 1; matrix products, arithmetic and copies ran while one was open for 0% -> 1% of each run, Pallas kernels for 0% -> 0%
where the time goes in v1:
time: 88.6 us; the launch traced here: 87.9 us
  blocking collectives  69.4 us (78%)
  starting transfers between devices  9.43 us (11%)
  local copies, waits for them, and re-layouts  3.83 us (4%)
  waiting for transfers between devices  2.36 us (3%)
  Pallas kernels  1.48 us (2%)
    all_gather x1, blocking collectives, per_device(): gathered = lax.all_gather(l_panel.T, ('slab', 'plane'), axis=0)  42.4 us
    all_to_all x1, blocking collectives, per_device(): lax.all_to_all(chunks.reshape((-1,) + masked.shape[1:]), ('half', 'twin')...  26.9 us
    all_to_all x1, starting transfers between devices, per_device(): inverse = lax.all_to_all(copies, 'x', 0, 0)  4.97 us
    all_to_all x1, starting transfers between devices, per_device(): shares = lax.all_to_all(partial.reshape(quads, width, order), QUAD, 0, 0)  4.45 us
    broadcast_in_dim x1, local copies, waits for them, and re-layouts, per_device(): jnp.broadcast_to(trailing_inverse[None], (lax.axis_size('x'),) + trailing...  2.66 us
    all_to_all x1, waiting for transfers between devices, per_device(): shares = lax.all_to_all(partial.reshape(quads, width, order), QUAD, 0, 0)  2.36 us
  transfers between devices with their start and end apart: 2, of which 1 were waited for; matrix products, arithmetic and copies ran while one was open for 1% of the time, Pallas kernels for 0%

profile of v1, /device:TPU:1, one launch (start us, length us, event | category | flops | bytes accessed | tf_op | source)
XLA Modules:
  0.0 87.9 jit_solution(8350960386558227143)
XLA Ops:
  0.0 2.7 %broadcast_in_dim.5 = bf16[4,256,1024]{2,1,0:T(8,128)(2,1)} broadcast(bf16[256,1024]{1,0:T(8,128)(2,1)} %param.3), dimensions={1,2} | broadcast | bytes 2621440 | tf_op jit(solution)/shard_map/broadcast_in_dim | solution.py:48
  2.7 0.0 copy-start.1
  2.7 0.0 copy-start
  2.7 5.0 %all-to-all-start.1 = ((bf16[4,256,1024]{2,1,0:T(8,128)(2,1)}), bf16[4,256,1024]{2,1,0:T(8,128)(2,1)S(1)}, u32[]{:S(2)}, u32[]{:S(2)}) async-start(bf16[4,256,1024]{2,1,0:T(8,128)(2,1)} %broadcast_in_dim.5), calls=%async_computation.1 | async-start | bytes 4194304 | tf_op jit(solution)/shard_map/all_to_all | solution.py:49
  7.6 0.0 copy-done.1
  7.7 0.1 reshape.29
  7.8 0.1 constant_dynamic-slice_fusion
  7.9 0.1 copy.13
  8.0 0.1 copy.11
  8.1 0.0 copy-done
  8.1 42.4 %all-gather = bf16[512,256]{1,0:T(8,128)(2,1)S(1)} all-gather(bf16[32,256]{1,0:T(8,128)(2,1)S(1)} %bitcast.15), channel_id=2, replica_groups=mesh['half'=2,'slab'=8,'plane'=2,'twin'=2,'x'=4,'y'=2,'core'=2] {'slab',..., dimensions={0}, use_global_device_ids=true | all-gather | bytes 278528 | tf_op jit(solution)/shard_map/all_gather | solution.py:50
  50.6 0.1 multiply_bitcast_fusion
  50.7 0.0 all-to-all-done.1.inverse_ref
  50.7 0.1 broadcast_in_dim.4
  50.8 26.9 %all_to_all.15 = bf16[16,2,2,32,256]{4,3,2,1,0:T(8,128)(2,1)S(1)} all-to-all(bf16[16,2,2,32,256]{4,3,2,1,0:T(8,128)(2,1)S(1)} %bitcast.13), channel_id=1, replica_groups=mesh['half'=2,'slab'=8,'plane'=2,'twin'=2,'x'=4,'y'=2,'core'=2] {'half',..., dimensions={0} | all-to-all | bytes 2097152 | tf_op jit(solution)/shard_map/all_to_all | solution.py:57
  77.8 1.5 %shard_map.37 = f32[128,256]{1,0:T(8,128)} custom-call(bf16[2,2,4,2,2,32,256]{6,5,4,3,2,1,0:T(8,128)(2,1)S(1)} %bitcast.12, bf16[4,256,1024]{2,1,0:T(8,128)(2,1)S(1)} %all-to-all-done.1.inverse_ref), custom_call_target="tpu_custom_call" | custom-call | flops 268435456 | bytes 3145728 | tf_op jit(solution)/shard_map/pallas_call | solution.py:28
  79.2 4.5 %all-to-all-start.2 = ((f32[4,32,256]{2,1,0:T(8,128)}), f32[4,32,256]{2,1,0:T(8,128)S(1)}, u32[]{:S(2)}, u32[]{:S(2)}) async-start(f32[4,32,256]{2,1,0:T(8,128)} %bitcast.6), calls=%async_computation.2 | async-start | bytes 262144 | tf_op jit(solution)/shard_map/all_to_all | solution.py:60
  83.7 0.6 dynamic_slice.12
  84.9 2.4 %all-to-all-done.2 = f32[4,32,256]{2,1,0:T(8,128)S(1)} async-done(((f32[4,32,256]{2,1,0:T(8,128)}), f32[4,32,256]{2,1,0:T(8,128)S(1)}, u32[]{:S(2)}, u32[]{:S(2)}) %all-to-all-start.2) | async-done | bytes 131104 | tf_op jit(solution)/shard_map/all_to_all | solution.py:60
  87.3 0.6 multiply_bitcast_fusion.1
  (4 shorter events, 0.1 us)
Async XLA Ops:
  2.7 5.0 %copy-start.1 = (s32[64,2]{0,1:T(2,128)S(1)}, s32[64,2]{0,1:T(2,128)}, u32[]{:S(2)}) copy-start(s32[64,2]{0,1:T(2,128)} %param.5) | copy-start | bytes 1540
  2.7 5.4 %copy-start = (bf16[256,32]{0,1:T(8,128)(2,1)S(1)}, bf16[256,32]{0,1:T(8,128)(2,1)}, u32[]{:S(2)}) copy-start(bf16[256,32]{0,1:T(8,128)(2,1)} %param.4) | copy-start | bytes 49156
  2.7 48.0 %all-to-all-start.1 = ((bf16[4,256,1024]{2,1,0:T(8,128)(2,1)}), bf16[4,256,1024]{2,1,0:T(8,128)(2,1)S(1)}, u32[]{:S(2)}, u32[]{:S(2)}) async-start(bf16[4,256,1024]{2,1,0:T(8,128)(2,1)} %broadcast_in_dim.5), calls=%async_computation.1 | async-start | bytes 4194304 | tf_op jit(solution)/shard_map/all_to_all | solution.py:49
  79.2 8.1 %all-to-all-start.2 = ((f32[4,32,256]{2,1,0:T(8,128)}), f32[4,32,256]{2,1,0:T(8,128)S(1)}, u32[]{:S(2)}, u32[]{:S(2)}) async-start(f32[4,32,256]{2,1,0:T(8,128)} %bitcast.6), calls=%async_computation.2 | async-start | bytes 262144 | tf_op jit(solution)/shard_map/all_to_all | solution.py:60

commit v2 on v1

--- a/solution.py
+++ b/solution.py
@@ -12,14 +12,14 @@
 
 def product(panel_ref, inverse_ref, out_ref):
     halves, twins, quads, planes, pairs, width, order = panel_ref.shape
-    total = jnp.zeros(out_ref.shape, jnp.float32)
+    total = jnp.zeros(out_ref.shape[::-1], jnp.float32)
     for half in range(halves):
         for pair in range(pairs):
             for plane in range(planes * twins):
                 left = panel_ref[half, plane % twins, :, plane // twins, pair].reshape(quads * width, order)
                 right = inverse_ref[half * pairs + pair, :, plane * order:(plane + 1) * order]
-                total += lax.dot_general(left, right, (((1,), (1,)), ((), ())), preferred_element_type=jnp.float32)
-    out_ref[...] = total
+                total += lax.dot_general(right, left, (((1,), (1,)), ((), ())), preferred_element_type=jnp.float32)
+    out_ref[...] = total.T
 
 
 def multiply(panel, inverse):
@@ -37,25 +37,66 @@
     )(panel, inverse)
 
 
+def copy_out(value_ref, out_ref, held_ref, load_sems, store_sems):
+    parts, count = load_sems.shape[0], out_ref.shape[0]
+    depth = value_ref.shape[0] // parts
+    spans = [pl.ds(i * depth, depth) for i in range(parts)]
+    loads = [pltpu.make_async_copy(value_ref.at[s], held_ref.at[s], load_sems.at[i]) for i, s in enumerate(spans)]
+    stores = [
+        [pltpu.make_async_copy(held_ref.at[s], out_ref.at[j, s], store_sems.at[i, j]) for j in range(count)]
+        for i, s in enumerate(spans)
+    ]
+    for load in loads:
+        load.start()
+    for load, group in zip(loads, stores):
+        load.wait()
+        for store in group:
+            store.start()
+    for group in stores:
+        for store in group:
+            store.wait()
+
+
+def repeat(value, count):
+    parts = 2
+    return pl.pallas_call(
+        copy_out,
+        in_specs=[pl.BlockSpec(memory_space=pl.ANY)],
+        out_specs=pl.BlockSpec(memory_space=pl.ANY),
+        out_shape=jax.ShapeDtypeStruct((count,) + value.shape, value.dtype),
+        scratch_shapes=[
+            pltpu.VMEM(value.shape, value.dtype),
+            pltpu.SemaphoreType.DMA((parts,)),
+            pltpu.SemaphoreType.DMA((parts, count)),
+        ],
+    )(value)
+
+
 def per_device(trailing_inverse, l_panel, pattern):
-    half, twin = lax.axis_index("half"), lax.axis_index("twin")
+    half, plane, twin = lax.axis_index("half"), lax.axis_index("plane"), lax.axis_index("twin")
     row, col = lax.axis_index(ROWS), lax.axis_index(COLS)
     halves, slabs, planes, twins = (lax.axis_size(a) for a in ROWS)
     cols, quads = lax.axis_size(COLS), lax.axis_size(QUAD)
+    core, cores, ys = lax.axis_index("core"), lax.axis_size("core"), lax.axis_size("y")
     pairs = slabs // quads
     order, width = l_panel.shape
     supernode = col * pattern.shape[1] // cols
-    copies = jnp.broadcast_to(trailing_inverse[None], (lax.axis_size("x"),) + trailing_inverse.shape)
+    copies = repeat(trailing_inverse, lax.axis_size("x"))
+    piece = l_panel.T
+    facing = lax.ppermute(piece, "plane", [(0, 1), (1, 0)])
+    copies, facing = lax.optimization_barrier((copies, facing))
     inverse = lax.all_to_all(copies, "x", 0, 0)
-    gathered = lax.all_gather(l_panel.T, ("slab", "plane"), axis=0)
-    gathered = gathered.reshape(pairs, quads, planes, width, order)
+    couple = jnp.where(plane == 0, jnp.stack([piece, facing]), jnp.stack([facing, piece]))
+    gathered = lax.all_gather(couple, ("slab", "core"), axis=0)
+    gathered = gathered.reshape(pairs, ys, cores, cores, planes, width, order)
+    gathered = lax.dynamic_index_in_dim(gathered, core, 2, keepdims=False)
     flags = lax.dynamic_index_in_dim(pattern, supernode, 1, keepdims=False)
-    flags = flags.reshape(halves, pairs, quads, planes, twins)[half, ..., twin]
-    masked = gathered * flags[..., None, None].astype(gathered.dtype)
-    masked = masked.transpose(1, 2, 0, 3, 4)
+    flags = flags.reshape(halves, pairs, ys, cores, planes, twins)[half, :, :, core, :, twin]
+    masked = gathered * flags[:, :, None, :, None, None].astype(gathered.dtype)
+    masked = masked.transpose(1, 2, 3, 0, 4, 5)
     chunks = jnp.broadcast_to(masked[None], (halves * twins,) + masked.shape)
-    panel = lax.all_to_all(chunks.reshape((-1,) + masked.shape[1:]), ("half", "twin") + QUAD, 0, 0)
-    panel = panel.reshape((halves, twins) + masked.shape)
+    panel = lax.all_to_all(chunks.reshape((-1,) + masked.shape[1:]), ("half", "twin", "y"), 0, 0)
+    panel = panel.reshape((halves, twins, quads) + masked.shape[2:])
     partial = multiply(panel, inverse)
     shares = lax.all_to_all(partial.reshape(quads, width, order), QUAD, 0, 0)
     mine = pattern[row, supernode]

time: 88.6 us -> 85.4 us (0.964)
  blocking collectives: 69.4 us -> 61.7 us
  starting transfers between devices: 9.43 us -> 14.7 us
  local copies, waits for them, and re-layouts: 3.83 us -> 0.87 us
  Pallas kernels: 1.48 us -> 3.78 us
    all_to_all x1, blocking collectives: 26.9 us -> 20.6 us  [per_device(): lax.all_to_all(chunks.reshape((-1,) + masked.shape[1:]), ('half', 'twin',...]
    ppermute x0 -> x1, starting transfers between devices: none -> 5.72 us  [per_device(): facing = lax.ppermute(piece, 'plane', [(0, 1), (1, 0)])]
    broadcast_in_dim x1 -> x0, local copies, waits for them, and re-layouts: 2.66 us -> none  [per_device(): jnp.broadcast_to(trailing_inverse[None], (lax.axis_size('x'),) + trailing...]
    pallas_call x0 -> x1, Pallas kernels: none -> 2.37 us  [repeat(): pl.pallas_call(copy_out, in_specs=[pl.BlockSpec(memory_space=pl.ANY)], ou...]
    all_gather x1, blocking collectives: 42.4 us -> 41.1 us  [per_device(): gathered = lax.all_gather(couple, ('slab', 'core'), axis=0)]
    all_to_all x1, starting transfers between devices: 4.97 us -> 4.02 us  [per_device(): inverse = lax.all_to_all(copies, 'x', 0, 0)]
  transfers between devices with their start and end apart: 2 -> 3, of which waited for: 1 -> 1; matrix products, arithmetic and copies ran while one was open for 1% -> 1% of each run, Pallas kernels for 0% -> 3%
where the time goes in v2:
time: 85.4 us; the launch traced here: 85.1 us
  blocking collectives  61.7 us (72%)
  starting transfers between devices  14.7 us (17%)
  Pallas kernels  3.78 us (4%)
  waiting for transfers between devices  2.37 us (3%)
  other arithmetic  0.9 us (1%)
  local copies, waits for them, and re-layouts  0.87 us (1%)
    all_gather x1, blocking collectives, per_device(): gathered = lax.all_gather(couple, ('slab', 'core'), axis=0)  41.1 us
    all_to_all x1, blocking collectives, per_device(): lax.all_to_all(chunks.reshape((-1,) + masked.shape[1:]), ('half', 'twin',...  20.6 us
    ppermute x1, starting transfers between devices, per_device(): facing = lax.ppermute(piece, 'plane', [(0, 1), (1, 0)])  5.72 us
    all_to_all x1, starting transfers between devices, per_device(): shares = lax.all_to_all(partial.reshape(quads, width, order), QUAD, 0, 0)  4.93 us
    all_to_all x1, starting transfers between devices, per_device(): inverse = lax.all_to_all(copies, 'x', 0, 0)  4.02 us
    pallas_call x1, Pallas kernels, repeat(): pl.pallas_call(copy_out, in_specs=[pl.BlockSpec(memory_space=pl.ANY)], ou...  2.37 us
    all_to_all x1, waiting for transfers between devices, per_device(): shares = lax.all_to_all(partial.reshape(quads, width, order), QUAD, 0, 0)  2.36 us
  transfers between devices with their start and end apart: 3, of which 1 were waited for; matrix products, arithmetic and copies ran while one was open for 1% of the time, Pallas kernels for 3%

profile of v2, /device:TPU:1, one launch (start us, length us, event | category | flops | bytes accessed | tf_op | source)
XLA Modules:
  0.0 85.1 jit_solution(4172459501349069668)
XLA Ops:
  0.0 5.7 %collective-permute-start = (bf16[32,256]{1,0:T(8,128)(2,1)}, bf16[32,256]{1,0:T(8,128)(2,1)S(1)}, u32[]{:S(2)}, u32[]{:S(2)}) collective-permute-start(bf16[32,256]{1,0:T(8,128)(2,1)} %bitcast.20), channel_id=1, source_target_pairs={{0,32},{32,0},{1,33},{33,1},{2,34},{34,2},{3,35},{35,3},{4,36},{36... | collective-permute-start | bytes 49160 | tf_op jit(solution)/shard_map/ppermute | solution.py:86
  5.7 2.4 %shard_map.37 = bf16[4,256,1024]{2,1,0:T(8,128)(2,1)} custom-call(bf16[256,1024]{1,0:T(8,128)(2,1)} %value_ref.1), custom_call_target="tpu_custom_call" | custom-call | tf_op jit(solution)/shard_map/pallas_call | solution.py:62
  8.1 0.0 copy-start.1
  8.1 0.0 copy-start
  8.1 0.0 collective-permute-done
  8.1 4.0 %all-to-all-start.1 = ((bf16[4,256,1024]{2,1,0:T(8,128)(2,1)}), bf16[4,256,1024]{2,1,0:T(8,128)(2,1)S(1)}, u32[]{:S(2)}, u32[]{:S(2)}) async-start(bf16[4,256,1024]{2,1,0:T(8,128)(2,1)} %shard_map.37), calls=%async_computation.1 | async-start | bytes 4194304 | tf_op jit(solution)/shard_map/all_to_all | solution.py:88
  12.2 0.0 copy-done.1
  12.2 0.1 reshape.87
  12.3 0.2 fusion.1
  12.5 0.0 copy-done
  12.5 41.1 %all_gather.4 = bf16[16,2,32,256]{3,2,1,0:T(8,128)(2,1)S(1)} all-gather(bf16[1,2,32,256]{3,2,1,0:T(8,128)(2,1)S(1)} %maximum_select_fusion), channel_id=1, replica_groups=mesh['half'=2,'slab'=8,'plane'=2,'twin'=2,'x'=4,'y'=2,'core'=2] {'slab',..., dimensions={0}, use_global_device_ids=true | all-gather | bytes 557056 | tf_op jit(solution)/shard_map/all_gather | solution.py:90
  53.6 0.1 fusion
  53.7 0.0 all-to-all-done.1.inverse_ref
  53.7 0.1 broadcast_in_dim.2
  53.9 20.6 %all_to_all.15 = bf16[8,2,2,2,32,256]{5,4,3,2,1,0:T(8,128)(2,1)S(1)} all-to-all(bf16[8,2,2,2,32,256]{5,4,3,2,1,0:T(8,128)(2,1)S(1)} %bitcast.18), channel_id=1, replica_groups=mesh['half'=2,'slab'=8,'plane'=2,'twin'=2,'x'=4,'y'=2,'core'=2] {'half',..., dimensions={0} | all-to-all | bytes 2097152 | tf_op jit(solution)/shard_map/all_to_all | solution.py:98
  74.5 1.4 %shard_map.38 = f32[128,256]{1,0:T(8,128)} custom-call(bf16[2,2,4,2,2,32,256]{6,5,4,3,2,1,0:T(8,128)(2,1)S(1)} %bitcast.17, bf16[4,256,1024]{2,1,0:T(8,128)(2,1)S(1)} %all-to-all-done.1.inverse_ref), custom_call_target="tpu_custom_call" | custom-call | flops 268435456 | bytes 3145728 | tf_op jit(solution)/shard_map/pallas_call | solution.py:28
  75.9 4.9 %all-to-all-start.2 = ((f32[4,32,256]{2,1,0:T(8,128)}), f32[4,32,256]{2,1,0:T(8,128)S(1)}, u32[]{:S(2)}, u32[]{:S(2)}) async-start(f32[4,32,256]{2,1,0:T(8,128)} %bitcast.9), calls=%async_computation.2 | async-start | bytes 262144 | tf_op jit(solution)/shard_map/all_to_all | solution.py:101
  80.8 0.6 dynamic_slice.17
  82.1 2.4 %all-to-all-done.2 = f32[4,32,256]{2,1,0:T(8,128)S(1)} async-done(((f32[4,32,256]{2,1,0:T(8,128)}), f32[4,32,256]{2,1,0:T(8,128)S(1)}, u32[]{:S(2)}, u32[]{:S(2)}) %all-to-all-start.2) | async-done | bytes 131104 | tf_op jit(solution)/shard_map/all_to_all | solution.py:101
  84.4 0.6 multiply_bitcast_fusion
  (4 shorter events, 0.1 us)
Async XLA Ops:
  0.0 8.1 %collective-permute-start = (bf16[32,256]{1,0:T(8,128)(2,1)}, bf16[32,256]{1,0:T(8,128)(2,1)S(1)}, u32[]{:S(2)}, u32[]{:S(2)}) collective-permute-start(bf16[32,256]{1,0:T(8,128)(2,1)} %bitcast.20), channel_id=1, source_target_pairs={{0,32},{32,0},{1,33},{33,1},{2,34},{34,2},{3,35},{35,3},{4,36},{36... | collective-permute-start | bytes 49160 | tf_op jit(solution)/shard_map/ppermute | solution.py:86
  8.1 4.1 %copy-start.1 = (s32[64,2]{0,1:T(2,128)S(1)}, s32[64,2]{0,1:T(2,128)}, u32[]{:S(2)}) copy-start(s32[64,2]{0,1:T(2,128)} %param.5) | copy-start | bytes 1540
  8.1 4.4 %copy-start = (bf16[256,32]{0,1:T(8,128)(2,1)S(1)}, bf16[256,32]{0,1:T(8,128)(2,1)}, u32[]{:S(2)}) copy-start(bf16[256,32]{0,1:T(8,128)(2,1)} %param.4) | copy-start | bytes 49156
  8.1 45.6 %all-to-all-start.1 = ((bf16[4,256,1024]{2,1,0:T(8,128)(2,1)}), bf16[4,256,1024]{2,1,0:T(8,128)(2,1)S(1)}, u32[]{:S(2)}, u32[]{:S(2)}) async-start(bf16[4,256,1024]{2,1,0:T(8,128)(2,1)} %shard_map.37), calls=%async_computation.1 | async-start | bytes 4194304 | tf_op jit(solution)/shard_map/all_to_all | solution.py:88
  75.9 8.5 %all-to-all-start.2 = ((f32[4,32,256]{2,1,0:T(8,128)}), f32[4,32,256]{2,1,0:T(8,128)S(1)}, u32[]{:S(2)}, u32[]{:S(2)}) async-start(f32[4,32,256]{2,1,0:T(8,128)} %bitcast.9), calls=%async_computation.2 | async-start | bytes 262144 | tf_op jit(solution)/shard_map/all_to_all | solution.py:101

commit v3 on v2

--- a/solution.py
+++ b/solution.py
@@ -10,31 +10,39 @@
 QUAD = ("y", "core")
 
 
-def product(panel_ref, inverse_ref, out_ref):
+def product(pattern_ref, panel_ref, inverse_ref, out_ref):
     halves, twins, quads, planes, pairs, width, order = panel_ref.shape
+    supernodes, cols = pattern_ref.shape[0], lax.axis_size(COLS)
+    supernode, quad = lax.axis_index(COLS) * supernodes // cols, lax.axis_index(QUAD)
     total = jnp.zeros(out_ref.shape[::-1], jnp.float32)
     for half in range(halves):
         for pair in range(pairs):
-            for plane in range(planes * twins):
-                left = panel_ref[half, plane % twins, :, plane // twins, pair].reshape(quads * width, order)
-                right = inverse_ref[half * pairs + pair, :, plane * order:(plane + 1) * order]
-                total += lax.dot_general(right, left, (((1,), (1,)), ((), ())), preferred_element_type=jnp.float32)
-    out_ref[...] = total.T
+            slab = (half * pairs + pair) * quads + quad
+            for plane in range(planes):
+                for twin in range(twins):
+                    step = plane * twins + twin
+                    keep = pattern_ref[supernode, slab * planes * twins + step]
+                    left = panel_ref[half, twin, :, plane, pair].reshape(quads * width, order)
+                    left = jnp.where(keep != 0, left, jnp.zeros_like(left))
+                    right = inverse_ref[half * pairs + pair, :, step * order:(step + 1) * order]
+                    total += lax.dot_general(right, left, (((1,), (1,)), ((), ())), preferred_element_type=jnp.float32)
+    mine = pattern_ref[supernode, lax.axis_index(ROWS)]
+    out_ref[...] = total.T * -mine.astype(jnp.float32)
 
 
-def multiply(panel, inverse):
+def multiply(pattern, panel, inverse):
     halves, twins, quads, planes, pairs, width, order = panel.shape
     vmem = pl.BlockSpec(memory_space=pltpu.VMEM)
     return pl.pallas_call(
         product,
-        in_specs=[vmem, vmem],
+        in_specs=[pl.BlockSpec(memory_space=pltpu.SMEM), vmem, vmem],
         out_specs=vmem,
         out_shape=jax.ShapeDtypeStruct((quads * width, order), jnp.float32),
         cost_estimate=pl.CostEstimate(
             flops=2 * panel.size * order, bytes_accessed=2 * (panel.size + inverse.size), transcendentals=0
         ),
         compiler_params=pltpu.CompilerParams(vmem_limit_bytes=16 * 1024 * 1024),
-    )(panel, inverse)
+    )(pattern.T, panel, inverse)
 
 
 def copy_out(value_ref, out_ref, held_ref, load_sems, store_sems):
@@ -73,14 +81,12 @@
 
 
 def per_device(trailing_inverse, l_panel, pattern):
-    half, plane, twin = lax.axis_index("half"), lax.axis_index("plane"), lax.axis_index("twin")
-    row, col = lax.axis_index(ROWS), lax.axis_index(COLS)
+    plane = lax.axis_index("plane")
     halves, slabs, planes, twins = (lax.axis_size(a) for a in ROWS)
-    cols, quads = lax.axis_size(COLS), lax.axis_size(QUAD)
+    quads = lax.axis_size(QUAD)
     core, cores, ys = lax.axis_index("core"), lax.axis_size("core"), lax.axis_size("y")
     pairs = slabs // quads
     order, width = l_panel.shape
-    supernode = col * pattern.shape[1] // cols
     copies = repeat(trailing_inverse, lax.axis_size("x"))
     piece = l_panel.T
     facing = lax.ppermute(piece, "plane", [(0, 1), (1, 0)])
@@ -90,17 +96,13 @@
     gathered = lax.all_gather(couple, ("slab", "core"), axis=0)
     gathered = gathered.reshape(pairs, ys, cores, cores, planes, width, order)
     gathered = lax.dynamic_index_in_dim(gathered, core, 2, keepdims=False)
-    flags = lax.dynamic_index_in_dim(pattern, supernode, 1, keepdims=False)
-    flags = flags.reshape(halves, pairs, ys, cores, planes, twins)[half, :, :, core, :, twin]
-    masked = gathered * flags[:, :, None, :, None, None].astype(gathered.dtype)
-    masked = masked.transpose(1, 2, 3, 0, 4, 5)
-    chunks = jnp.broadcast_to(masked[None], (halves * twins,) + masked.shape)
-    panel = lax.all_to_all(chunks.reshape((-1,) + masked.shape[1:]), ("half", "twin", "y"), 0, 0)
-    panel = panel.reshape((halves, twins, quads) + masked.shape[2:])
-    partial = multiply(panel, inverse)
+    pieces = gathered.transpose(1, 2, 3, 0, 4, 5)
+    chunks = jnp.broadcast_to(pieces[None], (halves * twins,) + pieces.shape)
+    panel = lax.all_to_all(chunks.reshape((-1,) + pieces.shape[1:]), ("half", "twin", "y"), 0, 0)
+    panel = panel.reshape((halves, twins, quads) + pieces.shape[2:])
+    partial = multiply(pattern, panel, inverse)
     shares = lax.all_to_all(partial.reshape(quads, width, order), QUAD, 0, 0)
-    mine = pattern[row, supernode]
-    return (jnp.sum(shares, 0) * -mine.astype(jnp.float32)).T
+    return jnp.sum(shares, 0).T
 
 
 def solution(mesh):

time: 85.4 us -> 84 us (0.984)
  blocking collectives: 61.7 us -> 69.4 us
  starting transfers between devices: 14.7 us -> 9.74 us
  waiting for transfers between devices: 2.37 us -> 0.01 us
    all_to_all x1 -> x2, blocking collectives: 20.6 us -> 28.2 us  [the longest x1 20.6 us: per_device(): lax.all_to_all(chunks.reshape((-1,) + pieces.shape[1:]), ('half', 'twin',...]
    all_to_all x1 -> x0, starting transfers between devices: 4.93 us -> none  [per_device(): shares = lax.all_to_all(partial.reshape(quads, width, order), QUAD, 0, 0)]
    all_to_all x1 -> x0, waiting for transfers between devices: 2.36 us -> none  [per_device(): shares = lax.all_to_all(partial.reshape(quads, width, order), QUAD, 0, 0)]
  transfers between devices with their start and end apart: 3 -> 2, of which waited for: 1 -> 0; matrix products, arithmetic and copies ran while one was open for 1% -> 0% of each run, Pallas kernels for 3% -> 3%
where the time goes in v3:
time: 84 us; the launch traced here: 83.7 us
  blocking collectives  69.4 us (83%)
  starting transfers between devices  9.74 us (12%)
  Pallas kernels  3.72 us (4%)
    all_gather x1, blocking collectives, per_device(): gathered = lax.all_gather(couple, ('slab', 'core'), axis=0)  41.1 us
    all_to_all x1, blocking collectives, per_device(): lax.all_to_all(chunks.reshape((-1,) + pieces.shape[1:]), ('half', 'twin',...  20.6 us
    all_to_all x1, blocking collectives, per_device(): shares = lax.all_to_all(partial.reshape(quads, width, order), QUAD, 0, 0)  7.62 us
    ppermute x1, starting transfers between devices, per_device(): facing = lax.ppermute(piece, 'plane', [(0, 1), (1, 0)])  5.72 us
    all_to_all x1, starting transfers between devices, per_device(): inverse = lax.all_to_all(copies, 'x', 0, 0)  4.02 us
    pallas_call x1, Pallas kernels, repeat(): pl.pallas_call(copy_out, in_specs=[pl.BlockSpec(memory_space=pl.ANY)], ou...  2.37 us
  transfers between devices with their start and end apart: 2, of which 0 were waited for; matrix products, arithmetic and copies ran while one was open for 0% of the time, Pallas kernels for 3%

profile of v3, /device:TPU:1, one launch (start us, length us, event | category | flops | bytes accessed | tf_op | source)
XLA Modules:
  0.0 83.7 jit_solution(13760647104150548616)
XLA Ops:
  0.0 5.7 %collective-permute-start = (bf16[32,256]{1,0:T(8,128)(2,1)}, bf16[32,256]{1,0:T(8,128)(2,1)S(1)}, u32[]{:S(2)}, u32[]{:S(2)}) collective-permute-start(bf16[32,256]{1,0:T(8,128)(2,1)} %bitcast.19), channel_id=1, source_target_pairs={{0,32},{32,0},{1,33},{33,1},{2,34},{34,2},{3,35},{35,3},{4,36},{36... | collective-permute-start | bytes 49160 | tf_op jit(solution)/shard_map/ppermute | solution.py:92
  5.7 2.4 %shard_map.37 = bf16[4,256,1024]{2,1,0:T(8,128)(2,1)} custom-call(bf16[256,1024]{1,0:T(8,128)(2,1)} %value_ref.1), custom_call_target="tpu_custom_call" | custom-call | tf_op jit(solution)/shard_map/pallas_call | solution.py:70
  8.1 0.0 copy-start.1
  8.1 0.0 collective-permute-done
  8.1 4.0 %all-to-all-start.1 = ((bf16[4,256,1024]{2,1,0:T(8,128)(2,1)}), bf16[4,256,1024]{2,1,0:T(8,128)(2,1)S(1)}, u32[]{:S(2)}, u32[]{:S(2)}) async-start(bf16[4,256,1024]{2,1,0:T(8,128)(2,1)} %shard_map.37), calls=%async_computation.1 | async-start | bytes 4194304 | tf_op jit(solution)/shard_map/all_to_all | solution.py:94
  12.2 0.0 copy-done.1
  12.2 41.1 %all_gather.4 = bf16[16,2,32,256]{3,2,1,0:T(8,128)(2,1)S(1)} all-gather(bf16[1,2,32,256]{3,2,1,0:T(8,128)(2,1)S(1)} %maximum_select_fusion), channel_id=1, replica_groups=mesh['half'=2,'slab'=8,'plane'=2,'twin'=2,'x'=4,'y'=2,'core'=2] {'slab',..., dimensions={0}, use_global_device_ids=true | all-gather | bytes 557056 | tf_op jit(solution)/shard_map/all_gather | solution.py:96
  53.3 0.0 copy-start
  53.4 0.0 all-to-all-done.1.inverse_ref
  53.4 0.1 broadcast_in_dim.2
  53.5 20.6 %all_to_all.15 = bf16[8,2,2,2,32,256]{5,4,3,2,1,0:T(8,128)(2,1)S(1)} all-to-all(bf16[8,2,2,2,32,256]{5,4,3,2,1,0:T(8,128)(2,1)S(1)} %bitcast.17), channel_id=1, replica_groups=mesh['half'=2,'slab'=8,'plane'=2,'twin'=2,'x'=4,'y'=2,'core'=2] {'half',..., dimensions={0} | all-to-all | bytes 2097152 | tf_op jit(solution)/shard_map/all_to_all | solution.py:101
  74.1 0.0 copy-done
  74.1 1.3 %shard_map.38 = f32[128,256]{1,0:T(8,128)S(1)} custom-call(s32[2,64]{1,0:T(2,128)S(1)} %bitcast.16, bf16[2,2,4,2,2,32,256]{6,5,4,3,2,1,0:T(8,128)(2,1)S(1)} %bitcast.14, bf16[4,256,1024]{2,1,0:T(8,128)(2,1)S(1)} %all-to-all-done.1.inverse_ref), custom_call_target="tpu_custom_call" | custom-call | flops 268435456 | bytes 3145728 | tf_op jit(solution)/shard_map/pallas_call | solution.py:36
  75.5 7.6 %all_to_all.16 = f32[4,32,256]{2,1,0:T(8,128)S(1)} all-to-all(f32[4,32,256]{2,1,0:T(8,128)S(1)} %bitcast.15), channel_id=1, replica_groups=mesh['half'=2,'slab'=8,'plane'=2,'twin'=2,'x'=4,'y'=2,'core'=2] {'y','co..., dimensions={0} | all-to-all | bytes 262144 | tf_op jit(solution)/shard_map/all_to_all | solution.py:104
  83.1 0.6 reduce_sum.9
  (3 shorter events, 0.0 us)
Async XLA Ops:
  0.0 8.1 %collective-permute-start = (bf16[32,256]{1,0:T(8,128)(2,1)}, bf16[32,256]{1,0:T(8,128)(2,1)S(1)}, u32[]{:S(2)}, u32[]{:S(2)}) collective-permute-start(bf16[32,256]{1,0:T(8,128)(2,1)} %bitcast.19), channel_id=1, source_target_pairs={{0,32},{32,0},{1,33},{33,1},{2,34},{34,2},{3,35},{35,3},{4,36},{36... | collective-permute-start | bytes 49160 | tf_op jit(solution)/shard_map/ppermute | solution.py:92
  8.1 4.0 %copy-start.1 = (bf16[256,32]{0,1:T(8,128)(2,1)S(1)}, bf16[256,32]{0,1:T(8,128)(2,1)}, u32[]{:S(2)}) copy-start(bf16[256,32]{0,1:T(8,128)(2,1)} %param.4) | copy-start | bytes 49156
  8.1 45.2 %all-to-all-start.1 = ((bf16[4,256,1024]{2,1,0:T(8,128)(2,1)}), bf16[4,256,1024]{2,1,0:T(8,128)(2,1)S(1)}, u32[]{:S(2)}, u32[]{:S(2)}) async-start(bf16[4,256,1024]{2,1,0:T(8,128)(2,1)} %shard_map.37), calls=%async_computation.1 | async-start | bytes 4194304 | tf_op jit(solution)/shard_map/all_to_all | solution.py:94
  53.3 20.8 %copy-start = (s32[64,2]{0,1:T(2,128)S(1)}, s32[64,2]{0,1:T(2,128)}, u32[]{:S(2)}) copy-start(s32[64,2]{0,1:T(2,128)} %param.5) | copy-start | bytes 1540

commit v4 on v3

--- a/solution.py
+++ b/solution.py
@@ -8,10 +8,14 @@
 ROWS = ("half", "slab", "plane", "twin")
 COLS = ("x", "y", "core")
 QUAD = ("y", "core")
+SHARE = ("twin", "y", "half")
 
 
 def product(pattern_ref, panel_ref, inverse_ref, out_ref):
-    halves, twins, quads, planes, pairs, width, order = panel_ref.shape
+    sizes = dict(zip(SHARE, panel_ref.shape))
+    halves, twins, ys = sizes["half"], sizes["twin"], sizes["y"]
+    cores, planes, pairs, width, order = panel_ref.shape[3:]
+    quads = ys * cores
     supernodes, cols = pattern_ref.shape[0], lax.axis_size(COLS)
     supernode, quad = lax.axis_index(COLS) * supernodes // cols, lax.axis_index(QUAD)
     total = jnp.zeros(out_ref.shape[::-1], jnp.float32)
@@ -22,7 +26,9 @@
                 for twin in range(twins):
                     step = plane * twins + twin
                     keep = pattern_ref[supernode, slab * planes * twins + step]
-                    left = panel_ref[half, twin, :, plane, pair].reshape(quads * width, order)
+                    places = [dict(half=half, twin=twin, y=y) for y in range(ys)]
+                    parts = [panel_ref[tuple(p[a] for a in SHARE) + (slice(None), plane, pair)] for p in places]
+                    left = jnp.concatenate([p.reshape(cores * width, order) for p in parts])
                     left = jnp.where(keep != 0, left, jnp.zeros_like(left))
                     right = inverse_ref[half * pairs + pair, :, step * order:(step + 1) * order]
                     total += lax.dot_general(right, left, (((1,), (1,)), ((), ())), preferred_element_type=jnp.float32)
@@ -31,7 +37,8 @@
 
 
 def multiply(pattern, panel, inverse):
-    halves, twins, quads, planes, pairs, width, order = panel.shape
+    width, order = panel.shape[-2:]
+    quads = lax.axis_size(QUAD)
     vmem = pl.BlockSpec(memory_space=pltpu.VMEM)
     return pl.pallas_call(
         product,
@@ -97,9 +104,10 @@
     gathered = gathered.reshape(pairs, ys, cores, cores, planes, width, order)
     gathered = lax.dynamic_index_in_dim(gathered, core, 2, keepdims=False)
     pieces = gathered.transpose(1, 2, 3, 0, 4, 5)
-    chunks = jnp.broadcast_to(pieces[None], (halves * twins,) + pieces.shape)
-    panel = lax.all_to_all(chunks.reshape((-1,) + pieces.shape[1:]), ("half", "twin", "y"), 0, 0)
-    panel = panel.reshape((halves, twins, quads) + pieces.shape[2:])
+    sizes = tuple(lax.axis_size(a) for a in SHARE)
+    chunks = jnp.broadcast_to(jnp.expand_dims(pieces, [i for i, a in enumerate(SHARE) if a != "y"]), sizes + pieces.shape[1:])
+    panel = lax.all_to_all(chunks.reshape((-1,) + pieces.shape[1:]), SHARE, 0, 0)
+    panel = panel.reshape(sizes + pieces.shape[1:])
     partial = multiply(pattern, panel, inverse)
     shares = lax.all_to_all(partial.reshape(quads, width, order), QUAD, 0, 0)
     return jnp.sum(shares, 0).T

time: 84 us -> 83.3 us (level)
  no operation moved by 1% of the time
where the time goes in v4:
time: 83.3 us; the launch traced here: 83 us
  blocking collectives  68.6 us (82%)
  starting transfers between devices  9.74 us (12%)
  Pallas kernels  3.71 us (4%)
    all_gather x1, blocking collectives, per_device(): gathered = lax.all_gather(couple, ('slab', 'core'), axis=0)  41.1 us
    all_to_all x1, blocking collectives, per_device(): lax.all_to_all(chunks.reshape((-1,) + pieces.shape[1:]), SHARE, 0, 0)  19.9 us
    all_to_all x1, blocking collectives, per_device(): shares = lax.all_to_all(partial.reshape(quads, width, order), QUAD, 0, 0)  7.61 us
    ppermute x1, starting transfers between devices, per_device(): facing = lax.ppermute(piece, 'plane', [(0, 1), (1, 0)])  5.72 us
    all_to_all x1, starting transfers between devices, per_device(): inverse = lax.all_to_all(copies, 'x', 0, 0)  4.02 us
    pallas_call x1, Pallas kernels, repeat(): pl.pallas_call(copy_out, in_specs=[pl.BlockSpec(memory_space=pl.ANY)], ou...  2.37 us
  transfers between devices with their start and end apart: 2, of which 0 were waited for; matrix products, arithmetic and copies ran while one was open for 0% of the time, Pallas kernels for 3%

profile of v4, /device:TPU:1, one launch (start us, length us, event | category | flops | bytes accessed | tf_op | source)
XLA Modules:
  0.0 83.0 jit_solution(1759296595727698506)
XLA Ops:
  0.0 5.7 %collective-permute-start = (bf16[32,256]{1,0:T(8,128)(2,1)}, bf16[32,256]{1,0:T(8,128)(2,1)S(1)}, u32[]{:S(2)}, u32[]{:S(2)}) collective-permute-start(bf16[32,256]{1,0:T(8,128)(2,1)} %bitcast.19), channel_id=1, source_target_pairs={{0,32},{32,0},{1,33},{33,1},{2,34},{34,2},{3,35},{35,3},{4,36},{36... | collective-permute-start | bytes 49160 | tf_op jit(solution)/shard_map/ppermute | solution.py:99
  5.7 2.4 %shard_map.37 = bf16[4,256,1024]{2,1,0:T(8,128)(2,1)} custom-call(bf16[256,1024]{1,0:T(8,128)(2,1)} %value_ref.1), custom_call_target="tpu_custom_call" | custom-call | tf_op jit(solution)/shard_map/pallas_call | solution.py:77
  8.1 0.0 copy-start.1
  8.1 0.0 collective-permute-done
  8.1 4.0 %all-to-all-start.1 = ((bf16[4,256,1024]{2,1,0:T(8,128)(2,1)}), bf16[4,256,1024]{2,1,0:T(8,128)(2,1)S(1)}, u32[]{:S(2)}, u32[]{:S(2)}) async-start(bf16[4,256,1024]{2,1,0:T(8,128)(2,1)} %shard_map.37), calls=%async_computation.1 | async-start | bytes 4194304 | tf_op jit(solution)/shard_map/all_to_all | solution.py:101
  12.2 0.0 copy-done.1
  12.2 41.1 %all_gather.4 = bf16[16,2,32,256]{3,2,1,0:T(8,128)(2,1)S(1)} all-gather(bf16[1,2,32,256]{3,2,1,0:T(8,128)(2,1)S(1)} %maximum_select_fusion), channel_id=1, replica_groups=mesh['half'=2,'slab'=8,'plane'=2,'twin'=2,'x'=4,'y'=2,'core'=2] {'slab',..., dimensions={0}, use_global_device_ids=true | all-gather | bytes 557056 | tf_op jit(solution)/shard_map/all_gather | solution.py:103
  53.3 0.0 copy-start
  53.4 0.0 all-to-all-done.1.inverse_ref
  53.4 0.1 broadcast_in_dim.2
  53.5 19.9 %all_to_all.15 = bf16[8,2,2,2,32,256]{5,4,3,2,1,0:T(8,128)(2,1)S(1)} all-to-all(bf16[8,2,2,2,32,256]{5,4,3,2,1,0:T(8,128)(2,1)S(1)} %bitcast.17), channel_id=1, replica_groups=mesh['half'=2,'slab'=8,'plane'=2,'twin'=2,'x'=4,'y'=2,'core'=2] {'twin',..., dimensions={0} | all-to-all | bytes 2097152 | tf_op jit(solution)/shard_map/all_to_all | solution.py:109
  73.4 0.0 copy-done
  73.4 1.3 %shard_map.38 = f32[128,256]{1,0:T(8,128)S(1)} custom-call(s32[2,64]{1,0:T(2,128)S(1)} %bitcast.16, bf16[2,2,2,2,2,2,32,256]{7,6,5,4,3,2,1,0:T(8,128)(2,1)S(1)} %bitcast.14, bf16[4,256,1024]{2,1,0:T(8,128)(2,1)S(1)} %all-to-all-done.1.inverse_ref), custom_call_target="tpu_custom_call" | custom-call | flops 268435456 | bytes 3145728 | tf_op jit(solution)/shard_map/pallas_call | solution.py:43
  74.8 7.6 %all_to_all.16 = f32[4,32,256]{2,1,0:T(8,128)S(1)} all-to-all(f32[4,32,256]{2,1,0:T(8,128)S(1)} %bitcast.15), channel_id=1, replica_groups=mesh['half'=2,'slab'=8,'plane'=2,'twin'=2,'x'=4,'y'=2,'core'=2] {'y','co..., dimensions={0} | all-to-all | bytes 262144 | tf_op jit(solution)/shard_map/all_to_all | solution.py:112
  82.4 0.6 reduce_sum.9
  (3 shorter events, 0.0 us)
Async XLA Ops:
  0.0 8.1 %collective-permute-start = (bf16[32,256]{1,0:T(8,128)(2,1)}, bf16[32,256]{1,0:T(8,128)(2,1)S(1)}, u32[]{:S(2)}, u32[]{:S(2)}) collective-permute-start(bf16[32,256]{1,0:T(8,128)(2,1)} %bitcast.19), channel_id=1, source_target_pairs={{0,32},{32,0},{1,33},{33,1},{2,34},{34,2},{3,35},{35,3},{4,36},{36... | collective-permute-start | bytes 49160 | tf_op jit(solution)/shard_map/ppermute | solution.py:99
  8.1 4.0 %copy-start.1 = (bf16[256,32]{0,1:T(8,128)(2,1)S(1)}, bf16[256,32]{0,1:T(8,128)(2,1)}, u32[]{:S(2)}) copy-start(bf16[256,32]{0,1:T(8,128)(2,1)} %param.4) | copy-start | bytes 49156
  8.1 45.2 %all-to-all-start.1 = ((bf16[4,256,1024]{2,1,0:T(8,128)(2,1)}), bf16[4,256,1024]{2,1,0:T(8,128)(2,1)S(1)}, u32[]{:S(2)}, u32[]{:S(2)}) async-start(bf16[4,256,1024]{2,1,0:T(8,128)(2,1)} %shard_map.37), calls=%async_computation.1 | async-start | bytes 4194304 | tf_op jit(solution)/shard_map/all_to_all | solution.py:101
  53.3 20.1 %copy-start = (s32[64,2]{0,1:T(2,128)S(1)}, s32[64,2]{0,1:T(2,128)}, u32[]{:S(2)}) copy-start(s32[64,2]{0,1:T(2,128)} %param.5) | copy-start | bytes 1540

commit v5 on v4

--- a/solution.py
+++ b/solution.py
@@ -18,6 +18,8 @@
     quads = ys * cores
     supernodes, cols = pattern_ref.shape[0], lax.axis_size(COLS)
     supernode, quad = lax.axis_index(COLS) * supernodes // cols, lax.axis_index(QUAD)
+    factors = jnp.where(supernode == 0, pattern_ref[0:1], pattern_ref[1:2])
+    lanes = lax.broadcasted_iota(jnp.int32, factors.shape, 1)
     total = jnp.zeros(out_ref.shape[::-1], jnp.float32)
     for half in range(halves):
         for pair in range(pairs):
@@ -25,14 +27,14 @@
             for plane in range(planes):
                 for twin in range(twins):
                     step = plane * twins + twin
-                    keep = pattern_ref[supernode, slab * planes * twins + step]
+                    keep = jnp.sum(jnp.where(lanes == slab * planes * twins + step, factors, 0), axis=1, keepdims=True)
                     places = [dict(half=half, twin=twin, y=y) for y in range(ys)]
                     parts = [panel_ref[tuple(p[a] for a in SHARE) + (slice(None), plane, pair)] for p in places]
                     left = jnp.concatenate([p.reshape(cores * width, order) for p in parts])
-                    left = jnp.where(keep != 0, left, jnp.zeros_like(left))
+                    left = left * keep.astype(left.dtype)
                     right = inverse_ref[half * pairs + pair, :, step * order:(step + 1) * order]
                     total += lax.dot_general(right, left, (((1,), (1,)), ((), ())), preferred_element_type=jnp.float32)
-    mine = pattern_ref[supernode, lax.axis_index(ROWS)]
+    mine = jnp.sum(jnp.where(lanes == lax.axis_index(ROWS), factors, 0), axis=1, keepdims=True)
     out_ref[...] = total.T * -mine.astype(jnp.float32)
 
 
@@ -42,7 +44,7 @@
     vmem = pl.BlockSpec(memory_space=pltpu.VMEM)
     return pl.pallas_call(
         product,
-        in_specs=[pl.BlockSpec(memory_space=pltpu.SMEM), vmem, vmem],
+        in_specs=[vmem, vmem, vmem],
         out_specs=vmem,
         out_shape=jax.ShapeDtypeStruct((quads * width, order), jnp.float32),
         cost_estimate=pl.CostEstimate(

time: 83.3 us -> 82.9 us (level)
  no operation moved by 1% of the time
where the time goes in v5:
time: 82.9 us; the launch traced here: 82.5 us
  blocking collectives  68.7 us (83%)
  starting transfers between devices  9.74 us (12%)
  Pallas kernels  3.25 us (4%)
    all_gather x1, blocking collectives, per_device(): gathered = lax.all_gather(couple, ('slab', 'core'), axis=0)  41.1 us
    all_to_all x1, blocking collectives, per_device(): lax.all_to_all(chunks.reshape((-1,) + pieces.shape[1:]), SHARE, 0, 0)  19.9 us
    all_to_all x1, blocking collectives, per_device(): shares = lax.all_to_all(partial.reshape(quads, width, order), QUAD, 0, 0)  7.62 us
    ppermute x1, starting transfers between devices, per_device(): facing = lax.ppermute(piece, 'plane', [(0, 1), (1, 0)])  5.72 us
    all_to_all x1, starting transfers between devices, per_device(): inverse = lax.all_to_all(copies, 'x', 0, 0)  4.02 us
    pallas_call x1, Pallas kernels, repeat(): pl.pallas_call(copy_out, in_specs=[pl.BlockSpec(memory_space=pl.ANY)], ou...  2.37 us
  transfers between devices with their start and end apart: 2, of which 0 were waited for; matrix products, arithmetic and copies ran while one was open for 0% of the time, Pallas kernels for 3%

profile of v5, /device:TPU:1, one launch (start us, length us, event | category | flops | bytes accessed | tf_op | source)
XLA Modules:
  0.0 82.5 jit_solution(11217713708888219456)
XLA Ops:
  0.0 5.7 %collective-permute-start = (bf16[32,256]{1,0:T(8,128)(2,1)}, bf16[32,256]{1,0:T(8,128)(2,1)S(1)}, u32[]{:S(2)}, u32[]{:S(2)}) collective-permute-start(bf16[32,256]{1,0:T(8,128)(2,1)} %bitcast.19), channel_id=1, source_target_pairs={{0,32},{32,0},{1,33},{33,1},{2,34},{34,2},{3,35},{35,3},{4,36},{36... | collective-permute-start | bytes 49160 | tf_op jit(solution)/shard_map/ppermute | solution.py:101
  5.7 2.4 %shard_map.37 = bf16[4,256,1024]{2,1,0:T(8,128)(2,1)} custom-call(bf16[256,1024]{1,0:T(8,128)(2,1)} %value_ref.1), custom_call_target="tpu_custom_call" | custom-call | tf_op jit(solution)/shard_map/pallas_call | solution.py:79
  8.1 0.0 copy-start.1
  8.1 0.0 collective-permute-done
  8.1 4.0 %all-to-all-start.1 = ((bf16[4,256,1024]{2,1,0:T(8,128)(2,1)}), bf16[4,256,1024]{2,1,0:T(8,128)(2,1)S(1)}, u32[]{:S(2)}, u32[]{:S(2)}) async-start(bf16[4,256,1024]{2,1,0:T(8,128)(2,1)} %shard_map.37), calls=%async_computation.1 | async-start | bytes 4194304 | tf_op jit(solution)/shard_map/all_to_all | solution.py:103
  12.2 0.0 copy-done.1
  12.2 41.1 %all_gather.4 = bf16[16,2,32,256]{3,2,1,0:T(8,128)(2,1)S(1)} all-gather(bf16[1,2,32,256]{3,2,1,0:T(8,128)(2,1)S(1)} %maximum_select_fusion), channel_id=1, replica_groups=mesh['half'=2,'slab'=8,'plane'=2,'twin'=2,'x'=4,'y'=2,'core'=2] {'slab',..., dimensions={0}, use_global_device_ids=true | all-gather | bytes 557056 | tf_op jit(solution)/shard_map/all_gather | solution.py:105
  53.3 0.0 copy-start
  53.4 0.0 all-to-all-done.1.inverse_ref
  53.4 0.1 broadcast_in_dim.2
  53.5 19.9 %all_to_all.15 = bf16[8,2,2,2,32,256]{5,4,3,2,1,0:T(8,128)(2,1)S(1)} all-to-all(bf16[8,2,2,2,32,256]{5,4,3,2,1,0:T(8,128)(2,1)S(1)} %bitcast.17), channel_id=1, replica_groups=mesh['half'=2,'slab'=8,'plane'=2,'twin'=2,'x'=4,'y'=2,'core'=2] {'twin',..., dimensions={0} | all-to-all | bytes 2097152 | tf_op jit(solution)/shard_map/all_to_all | solution.py:111
  73.4 0.0 copy-done
  73.4 0.9 %shard_map.38 = f32[128,256]{1,0:T(8,128)S(1)} custom-call(s32[2,64]{1,0:T(2,128)S(1)} %bitcast.16, bf16[2,2,2,2,2,2,32,256]{7,6,5,4,3,2,1,0:T(8,128)(2,1)S(1)} %bitcast.14, bf16[4,256,1024]{2,1,0:T(8,128)(2,1)S(1)} %all-to-all-done.1.inverse_ref), custom_call_target="tpu_custom_call" | custom-call | flops 268435456 | bytes 3145728 | tf_op jit(solution)/shard_map/pallas_call | solution.py:45
  74.3 7.6 %all_to_all.16 = f32[4,32,256]{2,1,0:T(8,128)S(1)} all-to-all(f32[4,32,256]{2,1,0:T(8,128)S(1)} %bitcast.15), channel_id=1, replica_groups=mesh['half'=2,'slab'=8,'plane'=2,'twin'=2,'x'=4,'y'=2,'core'=2] {'y','co..., dimensions={0} | all-to-all | bytes 262144 | tf_op jit(solution)/shard_map/all_to_all | solution.py:114
  81.9 0.6 reduce_sum.9
  (3 shorter events, 0.0 us)
Async XLA Ops:
  0.0 8.1 %collective-permute-start = (bf16[32,256]{1,0:T(8,128)(2,1)}, bf16[32,256]{1,0:T(8,128)(2,1)S(1)}, u32[]{:S(2)}, u32[]{:S(2)}) collective-permute-start(bf16[32,256]{1,0:T(8,128)(2,1)} %bitcast.19), channel_id=1, source_target_pairs={{0,32},{32,0},{1,33},{33,1},{2,34},{34,2},{3,35},{35,3},{4,36},{36... | collective-permute-start | bytes 49160 | tf_op jit(solution)/shard_map/ppermute | solution.py:101
  8.1 4.0 %copy-start.1 = (bf16[256,32]{0,1:T(8,128)(2,1)S(1)}, bf16[256,32]{0,1:T(8,128)(2,1)}, u32[]{:S(2)}) copy-start(bf16[256,32]{0,1:T(8,128)(2,1)} %param.4) | copy-start | bytes 49156
  8.1 45.2 %all-to-all-start.1 = ((bf16[4,256,1024]{2,1,0:T(8,128)(2,1)}), bf16[4,256,1024]{2,1,0:T(8,128)(2,1)S(1)}, u32[]{:S(2)}, u32[]{:S(2)}) async-start(bf16[4,256,1024]{2,1,0:T(8,128)(2,1)} %shard_map.37), calls=%async_computation.1 | async-start | bytes 4194304 | tf_op jit(solution)/shard_map/all_to_all | solution.py:103
  53.3 20.1 %copy-start = (s32[64,2]{0,1:T(2,128)S(1)}, s32[64,2]{0,1:T(2,128)}, u32[]{:S(2)}) copy-start(s32[64,2]{0,1:T(2,128)} %param.5) | copy-start | bytes 1540

commit v6 on v5

--- a/solution.py
+++ b/solution.py
@@ -24,16 +24,15 @@
     for half in range(halves):
         for pair in range(pairs):
             slab = (half * pairs + pair) * quads + quad
-            for plane in range(planes):
-                for twin in range(twins):
-                    step = plane * twins + twin
-                    keep = jnp.sum(jnp.where(lanes == slab * planes * twins + step, factors, 0), axis=1, keepdims=True)
-                    places = [dict(half=half, twin=twin, y=y) for y in range(ys)]
-                    parts = [panel_ref[tuple(p[a] for a in SHARE) + (slice(None), plane, pair)] for p in places]
-                    left = jnp.concatenate([p.reshape(cores * width, order) for p in parts])
-                    left = left * keep.astype(left.dtype)
-                    right = inverse_ref[half * pairs + pair, :, step * order:(step + 1) * order]
-                    total += lax.dot_general(right, left, (((1,), (1,)), ((), ())), preferred_element_type=jnp.float32)
+            pieces = []
+            for step in range(planes * twins):
+                keep = jnp.sum(jnp.where(lanes == slab * planes * twins + step, factors, 0), axis=1, keepdims=True)
+                places = [dict(half=half, twin=step % twins, y=y) for y in range(ys)]
+                at = (slice(None), step // twins, pair)
+                parts = [panel_ref[tuple(p[a] for a in SHARE) + at].reshape(cores * width, order) for p in places]
+                pieces.append(jnp.concatenate(parts) * keep.astype(panel_ref.dtype))
+            left, right = jnp.concatenate(pieces, axis=1), inverse_ref[half * pairs + pair]
+            total += lax.dot_general(right, left, (((1,), (1,)), ((), ())), preferred_element_type=jnp.float32)
     mine = jnp.sum(jnp.where(lanes == lax.axis_index(ROWS), factors, 0), axis=1, keepdims=True)
     out_ref[...] = total.T * -mine.astype(jnp.float32)
 

time: 82.9 us -> 82.9 us (level)
  no operation moved by 1% of the time
where the time goes in v6:
time: 82.9 us; the launch traced here: 82.5 us
  blocking collectives  68.6 us (83%)
  starting transfers between devices  9.74 us (12%)
  Pallas kernels  3.25 us (4%)
    all_gather x1, blocking collectives, per_device(): gathered = lax.all_gather(couple, ('slab', 'core'), axis=0)  41.1 us
    all_to_all x1, blocking collectives, per_device(): lax.all_to_all(chunks.reshape((-1,) + pieces.shape[1:]), SHARE, 0, 0)  19.9 us
    all_to_all x1, blocking collectives, per_device(): shares = lax.all_to_all(partial.reshape(quads, width, order), QUAD, 0, 0)  7.61 us
    ppermute x1, starting transfers between devices, per_device(): facing = lax.ppermute(piece, 'plane', [(0, 1), (1, 0)])  5.72 us
    all_to_all x1, starting transfers between devices, per_device(): inverse = lax.all_to_all(copies, 'x', 0, 0)  4.02 us
    pallas_call x1, Pallas kernels, repeat(): pl.pallas_call(copy_out, in_specs=[pl.BlockSpec(memory_space=pl.ANY)], ou...  2.37 us
  transfers between devices with their start and end apart: 2, of which 0 were waited for; matrix products, arithmetic and copies ran while one was open for 0% of the time, Pallas kernels for 3%

profile of v6, /device:TPU:1, one launch (start us, length us, event | category | flops | bytes accessed | tf_op | source)
XLA Modules:
  0.0 82.5 jit_solution(9481725963340683412)
XLA Ops:
  0.0 5.7 %collective-permute-start = (bf16[32,256]{1,0:T(8,128)(2,1)}, bf16[32,256]{1,0:T(8,128)(2,1)S(1)}, u32[]{:S(2)}, u32[]{:S(2)}) collective-permute-start(bf16[32,256]{1,0:T(8,128)(2,1)} %bitcast.19), channel_id=1, source_target_pairs={{0,32},{32,0},{1,33},{33,1},{2,34},{34,2},{3,35},{35,3},{4,36},{36... | collective-permute-start | bytes 49160 | tf_op jit(solution)/shard_map/ppermute | solution.py:100
  5.7 2.4 %shard_map.37 = bf16[4,256,1024]{2,1,0:T(8,128)(2,1)} custom-call(bf16[256,1024]{1,0:T(8,128)(2,1)} %value_ref.1), custom_call_target="tpu_custom_call" | custom-call | tf_op jit(solution)/shard_map/pallas_call | solution.py:78
  8.1 0.0 copy-start.1
  8.1 0.0 collective-permute-done
  8.1 4.0 %all-to-all-start.1 = ((bf16[4,256,1024]{2,1,0:T(8,128)(2,1)}), bf16[4,256,1024]{2,1,0:T(8,128)(2,1)S(1)}, u32[]{:S(2)}, u32[]{:S(2)}) async-start(bf16[4,256,1024]{2,1,0:T(8,128)(2,1)} %shard_map.37), calls=%async_computation.1 | async-start | bytes 4194304 | tf_op jit(solution)/shard_map/all_to_all | solution.py:102
  12.2 0.0 copy-done.1
  12.2 41.1 %all_gather.4 = bf16[16,2,32,256]{3,2,1,0:T(8,128)(2,1)S(1)} all-gather(bf16[1,2,32,256]{3,2,1,0:T(8,128)(2,1)S(1)} %maximum_select_fusion), channel_id=1, replica_groups=mesh['half'=2,'slab'=8,'plane'=2,'twin'=2,'x'=4,'y'=2,'core'=2] {'slab',..., dimensions={0}, use_global_device_ids=true | all-gather | bytes 557056 | tf_op jit(solution)/shard_map/all_gather | solution.py:104
  53.3 0.0 copy-start
  53.4 0.0 all-to-all-done.1.inverse_ref
  53.4 0.1 broadcast_in_dim.2
  53.5 19.9 %all_to_all.15 = bf16[8,2,2,2,32,256]{5,4,3,2,1,0:T(8,128)(2,1)S(1)} all-to-all(bf16[8,2,2,2,32,256]{5,4,3,2,1,0:T(8,128)(2,1)S(1)} %bitcast.17), channel_id=1, replica_groups=mesh['half'=2,'slab'=8,'plane'=2,'twin'=2,'x'=4,'y'=2,'core'=2] {'twin',..., dimensions={0} | all-to-all | bytes 2097152 | tf_op jit(solution)/shard_map/all_to_all | solution.py:110
  73.4 0.0 copy-done
  73.4 0.9 %shard_map.38 = f32[128,256]{1,0:T(8,128)S(1)} custom-call(s32[2,64]{1,0:T(2,128)S(1)} %bitcast.16, bf16[2,2,2,2,2,2,32,256]{7,6,5,4,3,2,1,0:T(8,128)(2,1)S(1)} %bitcast.14, bf16[4,256,1024]{2,1,0:T(8,128)(2,1)S(1)} %all-to-all-done.1.inverse_ref), custom_call_target="tpu_custom_call" | custom-call | flops 268435456 | bytes 3145728 | tf_op jit(solution)/shard_map/pallas_call | solution.py:44
  74.3 7.6 %all_to_all.16 = f32[4,32,256]{2,1,0:T(8,128)S(1)} all-to-all(f32[4,32,256]{2,1,0:T(8,128)S(1)} %bitcast.15), channel_id=1, replica_groups=mesh['half'=2,'slab'=8,'plane'=2,'twin'=2,'x'=4,'y'=2,'core'=2] {'y','co..., dimensions={0} | all-to-all | bytes 262144 | tf_op jit(solution)/shard_map/all_to_all | solution.py:113
  81.9 0.6 reduce_sum.9
  (3 shorter events, 0.0 us)
Async XLA Ops:
  0.0 8.1 %collective-permute-start = (bf16[32,256]{1,0:T(8,128)(2,1)}, bf16[32,256]{1,0:T(8,128)(2,1)S(1)}, u32[]{:S(2)}, u32[]{:S(2)}) collective-permute-start(bf16[32,256]{1,0:T(8,128)(2,1)} %bitcast.19), channel_id=1, source_target_pairs={{0,32},{32,0},{1,33},{33,1},{2,34},{34,2},{3,35},{35,3},{4,36},{36... | collective-permute-start | bytes 49160 | tf_op jit(solution)/shard_map/ppermute | solution.py:100
  8.1 4.0 %copy-start.1 = (bf16[256,32]{0,1:T(8,128)(2,1)S(1)}, bf16[256,32]{0,1:T(8,128)(2,1)}, u32[]{:S(2)}) copy-start(bf16[256,32]{0,1:T(8,128)(2,1)} %param.4) | copy-start | bytes 49156
  8.1 45.2 %all-to-all-start.1 = ((bf16[4,256,1024]{2,1,0:T(8,128)(2,1)}), bf16[4,256,1024]{2,1,0:T(8,128)(2,1)S(1)}, u32[]{:S(2)}, u32[]{:S(2)}) async-start(bf16[4,256,1024]{2,1,0:T(8,128)(2,1)} %shard_map.37), calls=%async_computation.1 | async-start | bytes 4194304 | tf_op jit(solution)/shard_map/all_to_all | solution.py:102
  53.3 20.1 %copy-start = (s32[64,2]{0,1:T(2,128)S(1)}, s32[64,2]{0,1:T(2,128)}, u32[]{:S(2)}) copy-start(s32[64,2]{0,1:T(2,128)} %param.5) | copy-start | bytes 1540
